TPU v7x, 256 devices: a whole 4x4x8 slice. The times are simulated.
256 devices in a mesh: seq: 64 (over z, x, core), head: 4 (over y).
Axes of the slice: x: 4, y: 4, z: 8, core: 2. Of those that a mesh axis runs over, the one named last changes fastest.
Arguments:
- video_q: bfloat16 [8192, 2048], P('seq', 'head'), may hold values from -7.5 to 7.5
- video_k: bfloat16 [8192, 2048], P('seq', 'head'), may hold values from -7.5 to 7.5
- video_v: bfloat16 [8192, 2048], P('seq', 'head'), may hold values from -24 to 24
- audio_q: bfloat16 [512, 2048], P('seq', 'head'), may hold values from -7.5 to 7.5
- audio_k: bfloat16 [512, 2048], P('seq', 'head'), may hold values from -7.5 to 7.5
- audio_v: bfloat16 [512, 2048], P('seq', 'head'), may hold values from -24 to 24
- video_lengths: int32 [4], replicated, may hold values from 1 to 3584, 8192 in all
- audio_lengths: int32 [4], replicated, may hold values from 1 to 224, 512 in all
- video_out_weight: bfloat16 [2048, 4096], P(None, 'head'), may hold values from -0.125 to 0.125
- audio_out_weight: bfloat16 [2048, 2048], P(None, 'head'), may hold values from -0.125 to 0.125
Outputs:
- video_out: bfloat16 [8192, 4096], P('seq', 'head')
- audio_out: bfloat16 [512, 2048], P('seq', 'head')
Inputs may be any that keep to these rules, and one draw needn't show every extreme that they name: `video_lengths`: clips lie end to end in order; one clip has exactly 3584 video tokens. `audio_lengths`: clips lie end to end in order; one clip has exactly 224 audio tokens.
All inputs are finite; a program needn't handle non-finite values.
Results may differ from a plain program's by a relative error of at most 0.012.
Values may be sent and summed in bfloat16 or wider, within the bound.
A program may use at most 64 MiB of HBM per device.

v0:
```python
import math
import jax
import jax.numpy as jnp
from jax import lax
from jax.sharding import Mesh
from jax.sharding import PartitionSpec as P

HEAD_DIM = 64
SEQ = ("seq_0", "seq_1", "seq_2")
masked_floor = -1e30


def sent_to_all(value, axis):
    count = lax.axis_size(axis)
    return lax.all_to_all(
        jnp.broadcast_to(value[None], (count, *value.shape)), axis, 0, 0, tiled=True
    )


def in_order(pieces, dim):
    pieces = jnp.moveaxis(pieces, 0, dim)
    dims = pieces.shape
    return pieces.reshape(*dims[:dim], dims[dim] * dims[dim + 1], *dims[dim + 2 :])


def gather_axes(value, axes, dim):
    far, near = axes
    first = sent_to_all(value, far)
    pieces = jnp.swapaxes(sent_to_all(first, near), 0, 1)
    return in_order(pieces.reshape(-1, *value.shape), dim)


def sent_together(arrays, axis, dim, along):
    both = jnp.concatenate(arrays, axis=along)
    filled, at, finished = (gather_axes(both, axis, dim), 0, [])
    for a in arrays:
        finished.append(lax.slice_in_dim(filled, at, at + a.shape[along], axis=along))
        at += a.shape[along]
    return tuple(finished)


def taken_together(value, axis):
    return sent_to_all(value, axis).max(axis=0)


def in_blocks(value, dim, count):
    dims = value.shape
    pieces = value.reshape(*dims[:dim], count, dims[dim] // count, *dims[dim + 1 :])
    return jnp.moveaxis(pieces, dim, 0)


def sum_at_owner(value, axis, dim):
    count = lax.axis_size(axis)
    pieces = lax.all_to_all(in_blocks(value, dim, count), axis, 0, 0, tiled=True)
    return jnp.sum(pieces, axis=0)


def sum_by_axis(value, axes, dim):
    far, near = axes
    own = sum_at_owner(in_blocks(value, dim, lax.axis_size(far)), near, dim + 1)
    return jnp.sum(lax.all_to_all(own, far, 0, 0, tiled=True), axis=0)


def sent_together_2(arrays, axis, dim, along):
    both = jnp.concatenate(arrays, axis=along)
    filled, at, finished = (sum_by_axis(both, axis, dim), 0, [])
    for a in arrays:
        finished.append(lax.slice_in_dim(filled, at, at + a.shape[along], axis=along))
        at += a.shape[along]
    return tuple(finished)


def gathered_copies(value, axis, dim):
    pieces = sent_to_all(value, axis)
    return in_order(pieces, dim)


def clip_index(positions, lengths):
    clip_ends = jnp.cumsum(lengths)
    return jnp.sum((positions[:, None] >= clip_ends[None, :]).astype(jnp.int32), axis=1)


def audio_clips(stored, audio_total, lengths):
    positions = (stored + audio_total // 2) % audio_total
    return clip_index(positions, lengths)


def per_device(
    video_q,
    video_k,
    video_v,
    audio_q,
    audio_k,
    audio_v,
    video_lengths,
    audio_lengths,
    video_out_weight,
    audio_out_weight,
):
    seq_count = lax.axis_size(SEQ)
    seq_rank = lax.axis_index(SEQ)
    video_rows, local_width = video_q.shape
    audio_rows = audio_q.shape[0]
    local_heads = local_width // HEAD_DIM
    audio_total = audio_rows * seq_count
    score_scale = 1.0 / math.sqrt(HEAD_DIM)
    video_clip = clip_index(
        seq_rank * video_rows + jnp.arange(video_rows, dtype=jnp.int32), video_lengths
    )
    query_clip = audio_clips(jnp.arange(audio_total, dtype=jnp.int32), audio_total, audio_lengths)
    every_query, every_key, every_value = sent_together(
        (audio_q, audio_k, audio_v), (("seq_0", "seq_1"), "seq_2"), 0, 1
    )
    query_heads = video_q.reshape(video_rows, local_heads, HEAD_DIM)
    scores = (
        jnp.einsum(
            "qhd,khd->qhk",
            query_heads,
            every_key.reshape(audio_total, local_heads, HEAD_DIM),
            preferred_element_type=jnp.float32,
        )
        * score_scale
    )
    allowed = video_clip[:, None, None] == query_clip[None, None, :]
    scores = jnp.where(allowed, scores, masked_floor)
    row_max = jnp.max(scores, axis=2, keepdims=True)
    weights = jnp.where(allowed, jnp.exp(scores - row_max), 0.0)
    video_totals = jnp.sum(weights, axis=2)
    video_mixed = jnp.einsum(
        "qhk,khd->qhd",
        weights.astype(jnp.bfloat16),
        every_value.reshape(audio_total, local_heads, HEAD_DIM),
        preferred_element_type=jnp.float32,
    )
    video_attn = (
        (video_mixed / video_totals[:, :, None])
        .reshape(video_rows, local_width)
        .astype(jnp.bfloat16)
    )
    video_proj = jnp.dot(
        lax.all_gather(video_attn, "head", axis=1, tiled=True),
        video_out_weight,
        preferred_element_type=jnp.float32,
    )
    query_block = math.gcd(audio_total, 512)
    block_count = audio_total // query_block
    video_key_heads = video_k.reshape(video_rows, local_heads, HEAD_DIM)
    video_value_heads = video_v.reshape(video_rows, local_heads, HEAD_DIM)

    def partial_block(paired):
        query_part, clip_part = paired
        block_scores = (
            jnp.einsum(
                "qhd,khd->qhk",
                query_part.reshape(query_block, local_heads, HEAD_DIM),
                video_key_heads,
                preferred_element_type=jnp.float32,
            )
            * score_scale
        )
        permitted = clip_part[:, None, None] == video_clip[None, None, :]
        block_scores = jnp.where(permitted, block_scores, masked_floor)
        local_max = jnp.max(block_scores, axis=2)
        block_weights = jnp.where(permitted, jnp.exp(block_scores - local_max[:, :, None]), 0.0)
        totals = jnp.sum(block_weights, axis=2)
        weighted = jnp.einsum(
            "qhk,khd->qhd",
            block_weights.astype(jnp.bfloat16),
            video_value_heads,
            preferred_element_type=jnp.float32,
        ).reshape(query_block, local_width)
        return (local_max, totals, weighted)

    local_max, totals, weighted = lax.map(
        partial_block,
        (
            every_query.reshape(block_count, query_block, local_width),
            query_clip.reshape(block_count, query_block),
        ),
    )
    local_max = local_max.reshape(audio_total, local_heads)
    totals = totals.reshape(audio_total, local_heads)
    weighted = weighted.reshape(audio_total, local_width)
    global_max = taken_together(local_max, SEQ)
    factor = jnp.exp(local_max - global_max)
    scaled_sum = (
        weighted.reshape(audio_total, local_heads, HEAD_DIM) * factor[:, :, None]
    ).reshape(audio_total, local_width)
    own_sum, own_total = sent_together_2(
        (scaled_sum, totals * factor), (("seq_0", "seq_1"), "seq_2"), 0, 1
    )
    audio_attn = (
        (own_sum.reshape(audio_rows, local_heads, HEAD_DIM) / own_total[:, :, None])
        .reshape(audio_rows, local_width)
        .astype(jnp.bfloat16)
    )
    audio_full = gathered_copies(audio_attn, "head", 1)
    audio_proj = jnp.dot(audio_full, audio_out_weight, preferred_element_type=jnp.float32)
    return (video_proj.astype(jnp.bfloat16), audio_proj.astype(jnp.bfloat16))


def solution(mesh):
    finer = Mesh(
        mesh.devices.reshape(8, 4, 2, mesh.shape["head"]), ("seq_0", "seq_1", "seq_2", "head")
    )
    placed = (
        P(SEQ, "head"),
        P(SEQ, "head"),
        P(SEQ, "head"),
        P(SEQ, "head"),
        P(SEQ, "head"),
        P(SEQ, "head"),
        P(),
        P(),
        P(None, "head"),
        P(None, "head"),
    )
    return jax.shard_map(
        per_device,
        mesh=finer,
        in_specs=placed,
        out_specs=(P(SEQ, "head"), P(SEQ, "head")),
        check_vma=False,
    )
```

profile of v0, /device:TPU:2, one launch (start us, length us, event | category | flops | bytes accessed | tf_op | source)
XLA Modules:
  0.0 135.7 jit_solution(13302887809576837175)
XLA Ops:
  2.5 11.6 %all-to-all-start = ((bf16[32,8,1536]{2,1,0:T(8,128)(2,1)}), bf16[32,8,1536]{2,1,0:T(8,128)(2,1)S(1)}, u32[]{:S(2)}, u32[]{:S(2)}) async-start(bf16[32,8,1536]{2,1,0:T(8,128)(2,1)} %broadcast_in_dim.91), calls=%async_computation | async-start | bytes 1572864 | tf_op jit(solution)/shard_map/all_to_all | solution.py:15
  15.0 21.6 %all-to-all-done = bf16[32,8,1536]{2,1,0:T(8,128)(2,1)S(1)} async-done(((bf16[32,8,1536]{2,1,0:T(8,128)(2,1)}), bf16[32,8,1536]{2,1,0:T(8,128)(2,1)S(1)}, u32[]{:S(2)}, u32[]{:S(2)}) %all-to-all-start) | async-done | bytes 786464 | tf_op jit(solution)/shard_map/all_to_all | solution.py:15
  36.7 5.0 %all_to_all.30 = bf16[2,32,8,1536]{3,2,1,0:T(8,128)(2,1)S(1)} all-to-all(bf16[2,32,8,1536]{3,2,1,0:T(8,128)(2,1)S(1)} %broadcast_in_dim.92), channel_id=1, replica_groups=mesh['seq_0'=8,'seq_1'=4,'seq_2'=2,'head'=4] {'seq_2'}, dimensions={0} | all-to-all | bytes 3145728 | tf_op jit(solution)/shard_map/all_to_all | solution.py:15
  41.9 1.1 fusion.36
  43.2 1.9 %bitcast_reduce_fusion = (f32[512,8]{0,1:T(8,128)S(1)}, f32[8,512,128]{2,1,0:T(8,128)}) fusion(pred[512,128]{1,0:T(8,128)(4,1)S(1)} %broadcast_compare_fusion, bf16[512,8,64]{0,2,1:T(8,128)(2,1)S(1)} %bitcast.66, bf16[128,8,64]{0,2,1:T(8,128)(2,1)S(1)} %bitcast.70), kind=kOutput, calls=%fused_computation.2 | convolution fusion | flops 68677632 | bytes 2834432 | tf_op jit(solution)/shard_map/while/body/eval_jaxpr/qhd,khd->qhk/dot_general | solution.py:153
  45.1 1.1 broadcast_in_dim.100
  46.2 6.0 %all-to-all-start.2 = ((f32[64,512,8]{1,2,0:T(8,128)}), f32[64,512,8]{1,2,0:T(8,128)S(1)}, u32[]{:S(2)}, u32[]{:S(2)}) async-start(f32[64,512,8]{1,2,0:T(8,128)} %broadcast_in_dim.100), calls=%async_computation.2 | async-start | bytes 2097152 | tf_op jit(solution)/shard_map/all_to_all | solution.py:15
  52.9 2.5 %fusion.4 = f32[512,8]{0,1:T(8,128)S(1)} fusion(f32[8,512,128]{2,1,0:T(8,128)} %get-tuple-element.26, f32[512,8]{0,1:T(8,128)S(1)} %get-tuple-element.25, pred[512,128]{1,0:T(8,128)(4,1)S(1)} %broadcast_compare_fusion), kind=kLoop, calls=%fused_computation.9 | loop fusion | flops 2617344 | bytes 2195456 | tf_op jit(solution)/shard_map/while/body/eval_jaxpr/reduce_sum | solution.py:165
  55.5 25.5 %all-to-all-done.2 = f32[64,512,8]{1,2,0:T(8,128)S(1)} async-done(((f32[64,512,8]{1,2,0:T(8,128)}), f32[64,512,8]{1,2,0:T(8,128)S(1)}, u32[]{:S(2)}, u32[]{:S(2)}) %all-to-all-start.2) | async-done | bytes 1048608 | tf_op jit(solution)/shard_map/all_to_all | solution.py:15
  81.2 2.3 %fusion.6 = f32[512,8,64]{0,2,1:T(8,128)S(1)} fusion(bf16[128,8,64]{0,2,1:T(8,128)(2,1)} %bitcast.76, f32[8,512,128]{2,1,0:T(8,128)} %get-tuple-element.26, f32[512,8]{0,1:T(8,128)S(1)} %get-tuple-element.25, pred[512,128]{1,0:T(8,128)(4,1)S(1)} %broadcast_compare_fusion, f32[512,8]{0,1:T(8,128)S(1)} %get-tuple-element.21), kind=kOutput, calls=%fused_computation.12 | convolution fusion | flops 69992448 | bytes 3375104 | tf_op jit(solution)/shard_map/while/body/eval_jaxpr/qhk,khd->qhd/dot_general | solution.py:166
  83.5 2.0 %copy.51 = f32[512,8,64]{2,1,0:T(8,128)} copy(f32[512,8,64]{0,2,1:T(8,128)S(1)} %fusion.6) | data formatting | bytes 2097152 | tf_op jit(solution)/shard_map/mul | solution.py:187
  85.5 1.9 %mul.52 = f32[32,2,8,512]{3,2,1,0:T(8,128)S(1)} reshape(f32[512,8,64]{2,1,0:T(8,128)} %copy.51) | data formatting | bytes 2097152 | tf_op jit(solution)/shard_map/mul | solution.py:187
  87.6 4.8 %all_to_all.31 = f32[2,32,8,520]{3,2,1,0:T(8,128)S(1)} all-to-all(f32[2,32,8,520]{3,2,1,0:T(8,128)S(1)} %copy.53), channel_id=1, replica_groups=mesh['seq_0'=8,'seq_1'=4,'seq_2'=2,'head'=4] {'seq_2'}, dimensions={0} | all-to-all | bytes 2129920 | tf_op jit(solution)/shard_map/all_to_all | solution.py:54
  92.4 1.0 reduce_sum.59
  93.4 5.4 %all-to-all-start.4 = ((f32[32,8,520]{2,1,0:T(8,128)}), f32[32,8,520]{2,1,0:T(8,128)S(1)}, u32[]{:S(2)}, u32[]{:S(2)}) async-start(f32[32,8,520]{2,1,0:T(8,128)} %reduce_sum.59), calls=%async_computation.4 | async-start | bytes 1310720 | tf_op jit(solution)/shard_map/all_to_all | solution.py:61
  99.7 2.1 %copy.43 = bf16[512,512]{0,1:T(8,128)(2,1)} copy(bf16[512,512]{1,0:T(8,128)(2,1)} %get-tuple-element.24) | data formatting | bytes 1048576 | tf_op jit(solution)/shard_map/slice | solution.py:37
  101.8 1.0 copy.44
  102.8 2.1 %fusion.37 = f32[128,8]{0,1:T(8,128)S(1)} fusion(pred[128,512]{0,1:T(8,128)(4,1)S(1)} %copy-done.6, bf16[512,8,64]{0,2,1:T(8,128)(2,1)} %bitcast.67, bf16[128,8,64]{0,2,1:T(8,128)(2,1)S(1)} %bitcast.72), kind=kOutput, calls=%fused_computation.54 | convolution fusion | flops 69730816 | bytes 724992 | tf_op jit(solution)/shard_map/sub | solution.py:127
  104.9 1.8 %fusion.38 = f32[8,512,128]{2,1,0:T(8,128)} fusion(bf16[512,8,64]{0,2,1:T(8,128)(2,1)S(1)} %bitcast.68, bf16[128,8,64]{0,2,1:T(8,128)(2,1)S(1)} %bitcast.73), kind=kOutput, calls=%fused_computation.55 | convolution fusion | flops 67108864 | bytes 2752512 | tf_op jit(solution)/shard_map/qhd,khd->qhk/dot_general | solution.py:116
  106.8 3.9 %fusion.8 = bf16[128,8,64]{0,2,1:T(8,128)(2,1)S(1)} fusion(bf16[512,8,64]{0,2,1:T(8,128)(2,1)} %bitcast.71, f32[8,512,128]{2,1,0:T(8,128)} %fusion.38, pred[128,512]{0,1:T(8,128)(4,1)S(1)} %copy-done.6, f32[128,8]{0,1:T(8,128)S(1)} %fusion.37), kind=kOutput, calls=%fused_computation.17 | convolution fusion | flops 69862912 | bytes 2822144 | tf_op jit(solution)/shard_map/qhk,khd->qhd/dot_general | solution.py:129
  110.6 13.3 %all_gather.3 = bf16[128,2048]{0,1:T(8,128)(2,1)S(1)} all-gather(bf16[128,512]{0,1:T(8,128)(2,1)S(1)} %bitcast.75), channel_id=1, replica_groups=mesh['seq_0'=8,'seq_1'=4,'seq_2'=2,'head'=4] {'head'}, dimensions={1}, use_global_device_ids=true | all-gather | bytes 655360 | tf_op jit(solution)/shard_map/all_gather | solution.py:141
  124.8 4.4 %all-to-all-start.5 = ((bf16[4,8,512]{2,1,0:T(8,128)(2,1)}), bf16[4,8,512]{2,1,0:T(8,128)(2,1)S(1)}, u32[]{:S(2)}, u32[]{:S(2)}) async-start(bf16[4,8,512]{2,1,0:T(8,128)(2,1)} %broadcast_in_dim.101), calls=%async_computation.5 | async-start | bytes 65536 | tf_op jit(solution)/shard_map/all_to_all | solution.py:15
  129.2 3.6 %convolution_convert_fusion = bf16[128,1024]{1,0:T(8,128)(2,1)} fusion(bf16[128,2048]{0,1:T(8,128)(2,1)S(1)} %all_gather.3, bf16[2048,1024]{1,0:T(8,128)(2,1)} %param.18), kind=kOutput, calls=%fused_computation.14 | convolution fusion | flops 537001984 | bytes 4980736 | tf_op jit(solution)/shard_map/dot_general | solution.py:140
  132.9 1.8 %all-to-all-done.5 = bf16[4,8,512]{2,1,0:T(8,128)(2,1)S(1)} async-done(((bf16[4,8,512]{2,1,0:T(8,128)(2,1)}), bf16[4,8,512]{2,1,0:T(8,128)(2,1)S(1)}, u32[]{:S(2)}, u32[]{:S(2)}) %all-to-all-start.5) | async-done | bytes 32800 | tf_op jit(solution)/shard_map/all_to_all | solution.py:15
  (47 shorter events, 7.1 us)
Async XLA Ops:
  0.6 134.0 %copy-start = (bf16[2048,512]{1,0:T(8,128)(2,1)S(1)}, bf16[2048,512]{1,0:T(8,128)(2,1)}, u32[]{:S(2)}) copy-start(bf16[2048,512]{1,0:T(8,128)(2,1)} %param.19) | copy-start | bytes 6291460
  0.6 13.5 %copy-start.7 = (s32[4]{0:T(128)S(1)}, s32[4]{0:T(128)}, u32[]{:S(2)}) copy-start(s32[4]{0:T(128)} %param.16) | copy-start | bytes 52
  0.7 13.7 %copy-start.8 = (s32[4]{0:T(128)S(1)}, s32[4]{0:T(128)}, u32[]{:S(2)}) copy-start(s32[4]{0:T(128)} %param.17) | copy-start | bytes 52
  0.7 13.8 %copy-start.3 = (bf16[128,512]{1,0:T(8,128)(2,1)S(1)}, bf16[128,512]{1,0:T(8,128)(2,1)}, u32[]{:S(2)}) copy-start(bf16[128,512]{1,0:T(8,128)(2,1)} %param.11) | copy-start | bytes 393220
  2.5 34.1 %all-to-all-start = ((bf16[32,8,1536]{2,1,0:T(8,128)(2,1)}), bf16[32,8,1536]{2,1,0:T(8,128)(2,1)S(1)}, u32[]{:S(2)}, u32[]{:S(2)}) async-start(bf16[32,8,1536]{2,1,0:T(8,128)(2,1)} %broadcast_in_dim.91), calls=%async_computation | async-start | bytes 1572864 | tf_op jit(solution)/shard_map/all_to_all | solution.py:15
  45.1 7.1 %copy-start.4 = (bf16[128,512]{1,0:T(8,128)(2,1)S(1)}, bf16[128,512]{1,0:T(8,128)(2,1)}, u32[]{:S(2)}) copy-start(bf16[128,512]{1,0:T(8,128)(2,1)} %param.12) | copy-start | bytes 393220
  46.2 34.8 %all-to-all-start.2 = ((f32[64,512,8]{1,2,0:T(8,128)}), f32[64,512,8]{1,2,0:T(8,128)S(1)}, u32[]{:S(2)}, u32[]{:S(2)}) async-start(f32[64,512,8]{1,2,0:T(8,128)} %broadcast_in_dim.100), calls=%async_computation.2 | async-start | bytes 2097152 | tf_op jit(solution)/shard_map/all_to_all | solution.py:15
  92.4 7.2 %copy-start.5 = (bf16[128,512]{1,0:T(8,128)(2,1)S(1)}, bf16[128,512]{1,0:T(8,128)(2,1)}, u32[]{:S(2)}) copy-start(bf16[128,512]{1,0:T(8,128)(2,1)} %param.10) | copy-start | bytes 393220
  93.4 8.4 %copy-start.1 = (bf16[512,512]{1,0:T(8,128)(2,1)S(1)}, bf16[512,512]{1,0:T(8,128)(2,1)}, u32[]{:S(2)}) copy-start(bf16[512,512]{1,0:T(8,128)(2,1)} %get-tuple-element.23) | copy-start | bytes 1572868
  93.4 30.5 %all-to-all-start.4 = ((f32[32,8,520]{2,1,0:T(8,128)}), f32[32,8,520]{2,1,0:T(8,128)S(1)}, u32[]{:S(2)}, u32[]{:S(2)}) async-start(f32[32,8,520]{2,1,0:T(8,128)} %reduce_sum.59), calls=%async_computation.4 | async-start | bytes 1310720 | tf_op jit(solution)/shard_map/all_to_all | solution.py:61
  99.7 3.1 %copy-start.6 = (pred[128,512]{0,1:T(8,128)(4,1)S(1)}, pred[128,512]{0,1:T(8,128)(4,1)}, u32[]{:S(2)}) copy-start(pred[128,512]{0,1:T(8,128)(4,1)} %broadcast_compare_fusion.1) | copy-start | bytes 196612
  102.8 2.1 %copy-start.2 = (bf16[512,512]{0,1:T(8,128)(2,1)S(1)}, bf16[512,512]{0,1:T(8,128)(2,1)}, u32[]{:S(2)}) copy-start(bf16[512,512]{0,1:T(8,128)(2,1)} %copy.44) | copy-start | bytes 1572868
  124.8 9.9 %all-to-all-start.5 = ((bf16[4,8,512]{2,1,0:T(8,128)(2,1)}), bf16[4,8,512]{2,1,0:T(8,128)(2,1)S(1)}, u32[]{:S(2)}, u32[]{:S(2)}) async-start(bf16[4,8,512]{2,1,0:T(8,128)(2,1)} %broadcast_in_dim.101), calls=%async_computation.5 | async-start | bytes 65536 | tf_op jit(solution)/shard_map/all_to_all | solution.py:15
where the time goes:
time: 136 us
  waiting for transfers between devices  48.9 us (36%)
  starting transfers between devices  27.4 us (20%)
  blocking collectives  23.1 us (17%)
  matrix products  16.6 us (12%)
  local copies, waits for them, and re-layouts  12.7 us (9%)
  other arithmetic  6.14 us (5%)
    all_to_all x3, waiting for transfers between devices, sent_to_all(): lax.all_to_all(jnp.broadcast_to(value[None], (count, *value.shape)), axis...  48.9 us
    all_to_all x3, starting transfers between devices, sent_to_all(): lax.all_to_all(jnp.broadcast_to(value[None], (count, *value.shape)), axis...  22 us
    all_gather x1, blocking collectives, per_device(): lax.all_gather(video_attn, 'head', axis=1, tiled=True)  13.3 us
    all_to_all x1, starting transfers between devices, sum_by_axis(): return jnp.sum(lax.all_to_all(own, far, 0, 0, tiled=True), axis=0)  5.38 us
    all_to_all x1, blocking collectives, sent_to_all(): lax.all_to_all(jnp.broadcast_to(value[None], (count, *value.shape)), axis...  5 us
    all_to_all x1, blocking collectives, sum_at_owner(): lax.all_to_all(in_blocks(value, dim, count), axis, 0, 0, tiled=True)  4.79 us
    slice x4, local copies, waits for them, and re-layouts, sent_together(): lax.slice_in_dim(filled, at, at + a.shape[along], axis=along)  4.41 us
    mul x2, local copies, waits for them, and re-layouts, per_device(): weighted.reshape(audio_total, local_heads, HEAD_DIM) * factor[:, :, None]  3.92 us
  transfers between devices with their start and end apart: 4, of which 3 were waited for; matrix products, arithmetic and copies ran while one was open for 14% of the time, Pallas kernels for 0%

commit v1 on v0

--- a/solution.py
+++ b/solution.py
@@ -4,6 +4,7 @@
 from jax import lax
 from jax.sharding import Mesh
 from jax.sharding import PartitionSpec as P
+from jax.lax import all_to_all, axis_size
 
 HEAD_DIM = 64
 SEQ = ("seq_0", "seq_1", "seq_2")
@@ -97,6 +98,12 @@
     video_out_weight,
     audio_out_weight,
 ):
+
+    def _carry_circles(inputs, d_out):
+        carry = jnp.stack(axis_size("head") * [inputs])
+        met_up = all_to_all(carry, axis_name="head", split_axis=0, concat_axis=0)
+        return jnp.concatenate(met_up, axis=d_out)
+
     seq_count = lax.axis_size(SEQ)
     seq_rank = lax.axis_index(SEQ)
     video_rows, local_width = video_q.shape
@@ -138,9 +145,7 @@
         .astype(jnp.bfloat16)
     )
     video_proj = jnp.dot(
-        lax.all_gather(video_attn, "head", axis=1, tiled=True),
-        video_out_weight,
-        preferred_element_type=jnp.float32,
+        _carry_circles(video_attn, 1), video_out_weight, preferred_element_type=jnp.float32
     )
     query_block = math.gcd(audio_total, 512)
     block_count = audio_total // query_block

time: 136 us -> 143 us (1.051)
  waiting for transfers between devices: 48.9 us -> 65.5 us
  blocking collectives: 23.1 us -> 9.78 us
  starting transfers between devices: 27.4 us -> 30.7 us
    all_gather x1 -> x0, blocking collectives: 13.3 us -> none  [per_device(): lax.all_gather(video_attn, 'head', axis=1, tiled=True)]
    all_to_all x1, waiting for transfers between devices: 0.01 us -> 8.77 us  [sum_by_axis(): return jnp.sum(lax.all_to_all(own, far, 0, 0, tiled=True), axis=0)]
    all_to_all x0 -> x1, waiting for transfers between devices: none -> 7.86 us  [_carry_circles(): met_up = all_to_all(carry, axis_name='head', split_axis=0, concat_axis=0)]
    all_to_all x0 -> x1, starting transfers between devices: none -> 4.46 us  [_carry_circles(): met_up = all_to_all(carry, axis_name='head', split_axis=0, concat_axis=0)]
  transfers between devices with their start and end apart: 4 -> 5, of which waited for: 3 -> 5; matrix products, arithmetic and copies ran while one was open for 14% -> 13% of each run, Pallas kernels for 0% -> 0%
where the time goes in v1:
time: 143 us; the launch traced here: 142 us
  waiting for transfers between devices  65.5 us (46%)
  starting transfers between devices  30.7 us (21%)
  matrix products  16.6 us (12%)
  local copies, waits for them, and re-layouts  13.5 us (9%)
  blocking collectives  9.78 us (7%)
  other arithmetic  5.52 us (4%)
    all_to_all x3, waiting for transfers between devices, sent_to_all(): lax.all_to_all(jnp.broadcast_to(value[None], (count, *value.shape)), axis...  48.9 us
    all_to_all x3, starting transfers between devices, sent_to_all(): lax.all_to_all(jnp.broadcast_to(value[None], (count, *value.shape)), axis...  20.8 us
    all_to_all x1, waiting for transfers between devices, sum_by_axis(): return jnp.sum(lax.all_to_all(own, far, 0, 0, tiled=True), axis=0)  8.77 us
    all_to_all x1, waiting for transfers between devices, _carry_circles(): met_up = all_to_all(carry, axis_name='head', split_axis=0, concat_axis=0)  7.86 us
    all_to_all x1, starting transfers between devices, sum_by_axis(): return jnp.sum(lax.all_to_all(own, far, 0, 0, tiled=True), axis=0)  5.38 us
    all_to_all x1, blocking collectives, sent_to_all(): lax.all_to_all(jnp.broadcast_to(value[None], (count, *value.shape)), axis...  5 us
    all_to_all x1, blocking collectives, sum_at_owner(): lax.all_to_all(in_blocks(value, dim, count), axis, 0, 0, tiled=True)  4.79 us
    all_to_all x1, starting transfers between devices, _carry_circles(): met_up = all_to_all(carry, axis_name='head', split_axis=0, concat_axis=0)  4.46 us
  transfers between devices with their start and end apart: 5, of which 5 were waited for; matrix products, arithmetic and copies ran while one was open for 13% of the time, Pallas kernels for 0%

profile of v1, /device:TPU:2, one launch (start us, length us, event | category | flops | bytes accessed | tf_op | source)
XLA Modules:
  0.0 142.4 jit_solution(1720540078618138357)
XLA Ops:
  2.5 11.6 %all-to-all-start = ((bf16[32,8,1536]{2,1,0:T(8,128)(2,1)}), bf16[32,8,1536]{2,1,0:T(8,128)(2,1)S(1)}, u32[]{:S(2)}, u32[]{:S(2)}) async-start(bf16[32,8,1536]{2,1,0:T(8,128)(2,1)} %broadcast_in_dim.91), calls=%async_computation | async-start | bytes 1572864 | tf_op jit(solution)/shard_map/all_to_all | solution.py:16
  15.0 21.6 %all-to-all-done = bf16[32,8,1536]{2,1,0:T(8,128)(2,1)S(1)} async-done(((bf16[32,8,1536]{2,1,0:T(8,128)(2,1)}), bf16[32,8,1536]{2,1,0:T(8,128)(2,1)S(1)}, u32[]{:S(2)}, u32[]{:S(2)}) %all-to-all-start) | async-done | bytes 786464 | tf_op jit(solution)/shard_map/all_to_all | solution.py:16
  36.7 5.0 %all_to_all.35 = bf16[2,32,8,1536]{3,2,1,0:T(8,128)(2,1)S(1)} all-to-all(bf16[2,32,8,1536]{3,2,1,0:T(8,128)(2,1)S(1)} %broadcast_in_dim.92), channel_id=1, replica_groups=mesh['seq_0'=8,'seq_1'=4,'seq_2'=2,'head'=4] {'seq_2'}, dimensions={0} | all-to-all | bytes 3145728 | tf_op jit(solution)/shard_map/all_to_all | solution.py:16
  41.9 1.1 fusion.36
  43.2 1.9 %bitcast_reduce_fusion = (f32[512,8]{0,1:T(8,128)S(1)}, f32[8,512,128]{2,1,0:T(8,128)}) fusion(pred[512,128]{1,0:T(8,128)(4,1)S(1)} %broadcast_compare_fusion, bf16[512,8,64]{0,2,1:T(8,128)(2,1)S(1)} %bitcast.70, bf16[128,8,64]{0,2,1:T(8,128)(2,1)S(1)} %bitcast.74), kind=kOutput, calls=%fused_computation.2 | convolution fusion | flops 68677632 | bytes 2834432 | tf_op jit(solution)/shard_map/while/body/eval_jaxpr/qhd,khd->qhk/dot_general | solution.py:158
  45.1 1.1 broadcast_in_dim.100
  46.2 6.0 %all-to-all-start.3 = ((f32[64,512,8]{1,2,0:T(8,128)}), f32[64,512,8]{1,2,0:T(8,128)S(1)}, u32[]{:S(2)}, u32[]{:S(2)}) async-start(f32[64,512,8]{1,2,0:T(8,128)} %broadcast_in_dim.100), calls=%async_computation.3 | async-start | bytes 2097152 | tf_op jit(solution)/shard_map/all_to_all | solution.py:16
  52.9 2.5 %fusion.4 = f32[512,8]{0,1:T(8,128)S(1)} fusion(f32[8,512,128]{2,1,0:T(8,128)} %get-tuple-element.26, f32[512,8]{0,1:T(8,128)S(1)} %get-tuple-element.25, pred[512,128]{1,0:T(8,128)(4,1)S(1)} %broadcast_compare_fusion), kind=kLoop, calls=%fused_computation.9 | loop fusion | flops 2617344 | bytes 2195456 | tf_op jit(solution)/shard_map/while/body/eval_jaxpr/reduce_sum | solution.py:170
  55.5 25.5 %all-to-all-done.3 = f32[64,512,8]{1,2,0:T(8,128)S(1)} async-done(((f32[64,512,8]{1,2,0:T(8,128)}), f32[64,512,8]{1,2,0:T(8,128)S(1)}, u32[]{:S(2)}, u32[]{:S(2)}) %all-to-all-start.3) | async-done | bytes 1048608 | tf_op jit(solution)/shard_map/all_to_all | solution.py:16
  81.2 2.3 %fusion.6 = f32[512,8,64]{0,2,1:T(8,128)S(1)} fusion(bf16[128,8,64]{0,2,1:T(8,128)(2,1)} %bitcast.80, f32[8,512,128]{2,1,0:T(8,128)} %get-tuple-element.26, f32[512,8]{0,1:T(8,128)S(1)} %get-tuple-element.25, pred[512,128]{1,0:T(8,128)(4,1)S(1)} %broadcast_compare_fusion, f32[512,8]{0,1:T(8,128)S(1)} %get-tuple-element.21), kind=kOutput, calls=%fused_computation.12 | convolution fusion | flops 69992448 | bytes 3375104 | tf_op jit(solution)/shard_map/while/body/eval_jaxpr/qhk,khd->qhd/dot_general | solution.py:171
  83.5 2.0 %copy.52 = f32[512,8,64]{2,1,0:T(8,128)} copy(f32[512,8,64]{0,2,1:T(8,128)S(1)} %fusion.6) | data formatting | bytes 2097152 | tf_op jit(solution)/shard_map/mul | solution.py:192
  85.5 1.9 %mul.52 = f32[32,2,8,512]{3,2,1,0:T(8,128)S(1)} reshape(f32[512,8,64]{2,1,0:T(8,128)} %copy.52) | data formatting | bytes 2097152 | tf_op jit(solution)/shard_map/mul | solution.py:192
  87.6 4.8 %all_to_all.36 = f32[2,32,8,520]{3,2,1,0:T(8,128)S(1)} all-to-all(f32[2,32,8,520]{3,2,1,0:T(8,128)S(1)} %copy.54), channel_id=1, replica_groups=mesh['seq_0'=8,'seq_1'=4,'seq_2'=2,'head'=4] {'seq_2'}, dimensions={0} | all-to-all | bytes 2129920 | tf_op jit(solution)/shard_map/all_to_all | solution.py:55
  93.4 5.4 %all-to-all-start.5 = ((f32[32,8,520]{2,1,0:T(8,128)}), f32[32,8,520]{2,1,0:T(8,128)S(1)}, u32[]{:S(2)}, u32[]{:S(2)}) async-start(f32[32,8,520]{2,1,0:T(8,128)} %reduce_sum.59), calls=%async_computation.5 | async-start | bytes 1310720 | tf_op jit(solution)/shard_map/all_to_all | solution.py:62
  99.1 2.1 %copy.44 = bf16[512,512]{0,1:T(8,128)(2,1)} copy(bf16[512,512]{1,0:T(8,128)(2,1)} %get-tuple-element.24) | data formatting | bytes 1048576 | tf_op jit(solution)/shard_map/slice | solution.py:38
  102.1 2.1 %fusion.37 = f32[128,8]{0,1:T(8,128)S(1)} fusion(pred[128,512]{0,1:T(8,128)(4,1)S(1)} %broadcast_compare_fusion.1, bf16[512,8,64]{0,2,1:T(8,128)(2,1)} %bitcast.71, bf16[128,8,64]{0,2,1:T(8,128)(2,1)S(1)} %bitcast.76), kind=kOutput, calls=%fused_computation.54 | convolution fusion | flops 69730816 | bytes 724992 | tf_op jit(solution)/shard_map/sub | solution.py:134
  104.3 1.8 %fusion.38 = f32[8,512,128]{2,1,0:T(8,128)} fusion(bf16[512,8,64]{0,2,1:T(8,128)(2,1)S(1)} %bitcast.72, bf16[128,8,64]{0,2,1:T(8,128)(2,1)S(1)} %bitcast.77), kind=kOutput, calls=%fused_computation.55 | convolution fusion | flops 67108864 | bytes 2752512 | tf_op jit(solution)/shard_map/qhd,khd->qhk/dot_general | solution.py:123
  106.1 3.9 %fusion.8 = bf16[128,8,64]{0,2,1:T(8,128)(2,1)S(1)} fusion(bf16[512,8,64]{0,2,1:T(8,128)(2,1)} %bitcast.75, f32[8,512,128]{2,1,0:T(8,128)} %fusion.38, pred[128,512]{0,1:T(8,128)(4,1)S(1)} %broadcast_compare_fusion.1, f32[128,8]{0,1:T(8,128)S(1)} %fusion.37), kind=kOutput, calls=%fused_computation.17 | convolution fusion | flops 69862912 | bytes 2822144 | tf_op jit(solution)/shard_map/qhk,khd->qhd/dot_general | solution.py:136
  110.0 8.8 %all-to-all-done.5 = f32[32,8,520]{2,1,0:T(8,128)S(1)} async-done(((f32[32,8,520]{2,1,0:T(8,128)}), f32[32,8,520]{2,1,0:T(8,128)S(1)}, u32[]{:S(2)}, u32[]{:S(2)}) %all-to-all-start.5) | async-done | bytes 532512 | tf_op jit(solution)/shard_map/all_to_all | solution.py:62
  119.6 4.5 %all-to-all-start.2 = ((bf16[4,128,512]{1,2,0:T(8,128)(2,1)}), bf16[4,128,512]{1,2,0:T(8,128)(2,1)S(1)}, u32[]{:S(2)}, u32[]{:S(2)}) async-start(bf16[4,128,512]{1,2,0:T(8,128)(2,1)} %stack.2), calls=%async_computation.2 | async-start | bytes 1048576 | tf_op jit(solution)/shard_map/all_to_all | solution.py:104
  124.3 7.9 %all-to-all-done.2 = bf16[4,128,512]{1,2,0:T(8,128)(2,1)S(1)} async-done(((bf16[4,128,512]{1,2,0:T(8,128)(2,1)}), bf16[4,128,512]{1,2,0:T(8,128)(2,1)S(1)}, u32[]{:S(2)}, u32[]{:S(2)}) %all-to-all-start.2) | async-done | bytes 524320 | tf_op jit(solution)/shard_map/all_to_all | solution.py:104
  132.8 3.3 %all-to-all-start.6 = ((bf16[4,8,512]{2,1,0:T(8,128)(2,1)}), bf16[4,8,512]{2,1,0:T(8,128)(2,1)S(1)}, u32[]{:S(2)}, u32[]{:S(2)}) async-start(bf16[4,8,512]{2,1,0:T(8,128)(2,1)} %broadcast_in_dim.101), calls=%async_computation.6 | async-start | bytes 65536 | tf_op jit(solution)/shard_map/all_to_all | solution.py:16
  136.0 3.6 %convolution_convert_fusion = bf16[128,1024]{1,0:T(8,128)(2,1)} fusion(bf16[128,2048]{0,1:T(8,128)(2,1)S(1)} %bitcast.69, bf16[2048,1024]{1,0:T(8,128)(2,1)} %param.18), kind=kOutput, calls=%fused_computation.14 | convolution fusion | flops 537001984 | bytes 4980736 | tf_op jit(solution)/shard_map/dot_general | solution.py:147
  139.7 1.8 %all-to-all-done.6 = bf16[4,8,512]{2,1,0:T(8,128)(2,1)S(1)} async-done(((bf16[4,8,512]{2,1,0:T(8,128)(2,1)}), bf16[4,8,512]{2,1,0:T(8,128)(2,1)S(1)}, u32[]{:S(2)}, u32[]{:S(2)}) %all-to-all-start.6) | async-done | bytes 32800 | tf_op jit(solution)/shard_map/all_to_all | solution.py:16
  (47 shorter events, 9.3 us)
Async XLA Ops:
  0.6 140.8 %copy-start = (bf16[2048,512]{1,0:T(8,128)(2,1)S(1)}, bf16[2048,512]{1,0:T(8,128)(2,1)}, u32[]{:S(2)}) copy-start(bf16[2048,512]{1,0:T(8,128)(2,1)} %param.19) | copy-start | bytes 6291460
  0.6 13.5 %copy-start.6 = (s32[4]{0:T(128)S(1)}, s32[4]{0:T(128)}, u32[]{:S(2)}) copy-start(s32[4]{0:T(128)} %param.16) | copy-start | bytes 52
  0.7 13.7 %copy-start.7 = (s32[4]{0:T(128)S(1)}, s32[4]{0:T(128)}, u32[]{:S(2)}) copy-start(s32[4]{0:T(128)} %param.17) | copy-start | bytes 52
  0.7 13.8 %copy-start.3 = (bf16[128,512]{1,0:T(8,128)(2,1)S(1)}, bf16[128,512]{1,0:T(8,128)(2,1)}, u32[]{:S(2)}) copy-start(bf16[128,512]{1,0:T(8,128)(2,1)} %param.11) | copy-start | bytes 393220
  2.5 34.1 %all-to-all-start = ((bf16[32,8,1536]{2,1,0:T(8,128)(2,1)}), bf16[32,8,1536]{2,1,0:T(8,128)(2,1)S(1)}, u32[]{:S(2)}, u32[]{:S(2)}) async-start(bf16[32,8,1536]{2,1,0:T(8,128)(2,1)} %broadcast_in_dim.91), calls=%async_computation | async-start | bytes 1572864 | tf_op jit(solution)/shard_map/all_to_all | solution.py:16
  45.1 7.1 %copy-start.4 = (bf16[128,512]{1,0:T(8,128)(2,1)S(1)}, bf16[128,512]{1,0:T(8,128)(2,1)}, u32[]{:S(2)}) copy-start(bf16[128,512]{1,0:T(8,128)(2,1)} %param.12) | copy-start | bytes 393220
  46.2 34.8 %all-to-all-start.3 = ((f32[64,512,8]{1,2,0:T(8,128)}), f32[64,512,8]{1,2,0:T(8,128)S(1)}, u32[]{:S(2)}, u32[]{:S(2)}) async-start(f32[64,512,8]{1,2,0:T(8,128)} %broadcast_in_dim.100), calls=%async_computation.3 | async-start | bytes 2097152 | tf_op jit(solution)/shard_map/all_to_all | solution.py:16
  92.4 6.4 %copy-start.5 = (bf16[128,512]{1,0:T(8,128)(2,1)S(1)}, bf16[128,512]{1,0:T(8,128)(2,1)}, u32[]{:S(2)}) copy-start(bf16[128,512]{1,0:T(8,128)(2,1)} %param.10) | copy-start | bytes 393220
  93.4 7.7 %copy-start.1 = (bf16[512,512]{1,0:T(8,128)(2,1)S(1)}, bf16[512,512]{1,0:T(8,128)(2,1)}, u32[]{:S(2)}) copy-start(bf16[512,512]{1,0:T(8,128)(2,1)} %get-tuple-element.23) | copy-start | bytes 1572868
  93.4 25.3 %all-to-all-start.5 = ((f32[32,8,520]{2,1,0:T(8,128)}), f32[32,8,520]{2,1,0:T(8,128)S(1)}, u32[]{:S(2)}, u32[]{:S(2)}) async-start(f32[32,8,520]{2,1,0:T(8,128)} %reduce_sum.59), calls=%async_computation.5 | async-start | bytes 1310720 | tf_op jit(solution)/shard_map/all_to_all | solution.py:62
  102.1 2.1 %copy-start.2 = (bf16[512,512]{0,1:T(8,128)(2,1)S(1)}, bf16[512,512]{0,1:T(8,128)(2,1)}, u32[]{:S(2)}) copy-start(bf16[512,512]{0,1:T(8,128)(2,1)} %copy.45) | copy-start | bytes 1572868
  119.6 12.5 %all-to-all-start.2 = ((bf16[4,128,512]{1,2,0:T(8,128)(2,1)}), bf16[4,128,512]{1,2,0:T(8,128)(2,1)S(1)}, u32[]{:S(2)}, u32[]{:S(2)}) async-start(bf16[4,128,512]{1,2,0:T(8,128)(2,1)} %stack.2), calls=%async_computation.2 | async-start | bytes 1048576 | tf_op jit(solution)/shard_map/all_to_all | solution.py:104
  132.8 8.7 %all-to-all-start.6 = ((bf16[4,8,512]{2,1,0:T(8,128)(2,1)}), bf16[4,8,512]{2,1,0:T(8,128)(2,1)S(1)}, u32[]{:S(2)}, u32[]{:S(2)}) async-start(bf16[4,8,512]{2,1,0:T(8,128)(2,1)} %broadcast_in_dim.101), calls=%async_computation.6 | async-start | bytes 65536 | tf_op jit(solution)/shard_map/all_to_all | solution.py:16
